TPU v7x, 512 devices: a whole 4x4x16 slice. The times are simulated.
512 devices in a mesh: dp: 16 (over y, x), fsdp: 32 (over z, core).
Axes of the slice: x: 4, y: 4, z: 16, core: 2. Of those that a mesh axis runs over, the one named last changes fastest.
Arguments:
- projections: bfloat16 [65536, 3, 2048], P(('dp', 'fsdp')), parts along dimension 0, may hold values from -6 to 6
- positions: int32 [3, 65536], P(None, ('dp', 'fsdp')), parts along dimension 1, may hold values from 0 to 63
- packed_index: int32 [65536], P(('dp', 'fsdp')), parts along dimension 0, may hold values from 0 to 4095, as said below
- clip_length: int32 [384], P('dp'), parts along dimension 0, may hold values from 64 to 832, as said below
- clip_group: int32 [384], P('dp'), parts along dimension 0, may hold values from 0 to 5, as said below
- query_gain: float32 [128], replicated, may hold values from 0.5 to 1.5
- key_gain: float32 [128], replicated, may hold values from 0.5 to 1.5
- out_weight: bfloat16 [2048, 1536], P('fsdp'), may hold values from -1 to 1
Outputs:
- mixed_rows: bfloat16 [65536, 1536], P(('dp', 'fsdp')), parts along dimension 0
There are 16 independent parts, one for each index of `dp`. A program takes and returns all parts, laid end to end along the dimension named above; an argument that names none is the same for every part. Nothing has to cross between parts.
Inputs may be any that keep to these rules, and one draw needn't show every extreme that they name: `packed_index`: A permutation of the packed positions; the 128 rows of each aligned block send exactly 4 rows to each aligned block of 128 packed positions. `clip_group`: each sequence group is named by exactly 4 clips. `clip_length`: the clips of a group add up to that group's packed positions.
All inputs are finite; a program needn't handle non-finite values.
Results may differ from a plain program's by a relative error of at most 0.0071.
Values may be sent and summed in bfloat16 or wider, within the bound.
A program may use at most 64 MiB of HBM per device.

v0:
```python
import math

import jax
import jax.numpy as jnp
import numpy as np
from jax import lax
from jax.sharding import PartitionSpec as P

HD = 128
CPG = 4


ROPE_BASE = 256.0
NORM_EPS = 1e-06


def partner(value, axis, apart):
    return lax.ppermute(value, axis, [(i, i ^ 1 << apart) for i in range(lax.axis_size(axis))])


def rope_tables(head_width):
    lead_width = head_width // 8
    side_width = (head_width - lead_width) // 2
    axis_list, freq_list, partner_list, sign_list = ([], [], [], [])
    offset = 0
    for axis_number, section in enumerate([lead_width, side_width, side_width]):
        middle = section // 2
        for column in range(section):
            within = column % middle
            axis_list.append(axis_number)
            freq_list.append(ROPE_BASE ** (-2.0 * within / section))
            if column < middle:
                partner_list.append(offset + column + middle)
                sign_list.append(-1.0)
            else:
                partner_list.append(offset + column - middle)
                sign_list.append(1.0)
        offset += section
    return (
        np.array(axis_list, np.int32),
        np.array(freq_list, np.float32),
        np.array(partner_list, np.int32),
        np.array(sign_list, np.float32),
    )


def rotate_heads(projections, positions, query_gain, key_gain):
    row_count = projections.shape[0]
    head_count = projections.shape[2] // HD
    axis_table, freq_table, partner_table, sign_table = rope_tables(HD)
    angles = positions.astype(jnp.float32)[axis_table, :].T * freq_table[None, :]
    cosine = jnp.cos(angles)[:, None, :]
    sine_part = jnp.sin(angles)[:, None, :]

    def normed(entries, gain):
        entries = entries.astype(jnp.float32).reshape(row_count, head_count, HD)
        factor = lax.rsqrt(jnp.mean(entries * entries, axis=-1, keepdims=True) + NORM_EPS)
        entries = entries * factor * gain
        turned = entries * cosine + entries[..., partner_table] * sign_table * sine_part
        return turned.reshape(row_count, head_count * HD).astype(jnp.bfloat16)

    return (normed(projections[:, 0], query_gain), normed(projections[:, 1], key_gain))


def clip_ends(group_id, clip_length, clip_group):
    count = clip_length.shape[0]
    clip_ids = jnp.arange(count, dtype=jnp.int32)
    inside = clip_group == group_id
    earlier = inside[None, :] & (clip_ids[None, :] <= clip_ids[:, None])
    ends = jnp.sum(jnp.where(earlier, clip_length[None, :], 0), axis=1)
    return jnp.where(inside, ends, jnp.int32(1 << 30))


def group_shape(device, device_count):
    halfway = device_count // 2
    big_size = min(8, halfway)
    is_wide = device < halfway
    group_size = jnp.where(is_wide, big_size, 4)
    group_start = device - device % group_size
    group_id = jnp.where(is_wide, device // big_size, halfway // big_size + (device - halfway) // 4)
    return (group_size, group_start, group_id)


def butterfly(blocks, group_rank, is_wide, swapper):
    for bit_number in range(3):
        axis_number = 2 - bit_number
        bit_clear = group_rank >> bit_number & 1 == 0
        first_half = jnp.take(blocks, 0, axis=axis_number)
        second_half = jnp.take(blocks, 1, axis=axis_number)
        kept_half = jnp.where(bit_clear, first_half, second_half)
        leaving = jnp.where(bit_clear, second_half, first_half)
        arrived = swapper(leaving, bit_number)
        merged = jnp.stack(
            [jnp.where(bit_clear, kept_half, arrived), jnp.where(bit_clear, arrived, kept_half)],
            axis=axis_number,
        )
        if bit_number == 2:
            merged = jnp.where(is_wide, merged, blocks)
        blocks = merged
    return blocks


def attend(stacked, labels, unit_heads):
    row_total = stacked.shape[0]
    block_rows = min(512, row_total)
    score_scale = 1.0 / math.sqrt(HD)
    queries = stacked[:, 0].reshape(row_total, unit_heads, HD)
    key_rows = stacked[:, 1].reshape(row_total, unit_heads, HD)
    value_rows = stacked[:, 2].reshape(row_total, unit_heads, HD)

    def one_block(block_index):
        first_row = block_index * block_rows
        query_block = lax.dynamic_slice_in_dim(queries, first_row, block_rows, 0)
        label_block = lax.dynamic_slice_in_dim(labels, first_row, block_rows, 0)
        scores = (
            jnp.einsum("qhd,khd->hqk", query_block, key_rows, preferred_element_type=jnp.float32)
            * score_scale
        )
        allowed = label_block[:, None] == labels[None, :]
        weights = jnp.where(allowed[None], jnp.exp(scores), 0.0)
        weights = (weights / jnp.sum(weights, axis=-1, keepdims=True)).astype(jnp.bfloat16)
        result = jnp.einsum("hqk,khd->qhd", weights, value_rows, preferred_element_type=jnp.float32)
        return result.astype(jnp.bfloat16).reshape(block_rows, unit_heads * HD)

    pieces = lax.map(one_block, jnp.arange(row_total // block_rows))
    return pieces.reshape(row_total, unit_heads * HD)


def on_device(
    projections, positions, packed_index, clip_length, clip_group, query_gain, key_gain, out_weight
):
    row_count = projections.shape[0]
    device_count = lax.axis_size("fsdp")
    device = lax.axis_index("fsdp")
    peer_rows = row_count // device_count
    head_width = projections.shape[2]
    unit_width = head_width // 8
    unit_heads = unit_width // HD
    group_size, group_start, group_id = group_shape(device, device_count)
    ends = clip_ends(group_id, clip_length, clip_group)
    flat_ids = jnp.arange(8 * row_count, dtype=jnp.int32)
    capacity = group_size * row_count
    within_group = flat_ids % capacity
    finished = jnp.sum((within_group[:, None] >= ends[None, :]).astype(jnp.int32), axis=1)
    labels = flat_ids // capacity * CPG + finished
    rotated_query, rotated_key = rotate_heads(projections, positions, query_gain, key_gain)
    stacked = jnp.stack([rotated_query, rotated_key, projections[:, 2]], axis=1)
    target_device = packed_index // row_count
    send_order = jnp.argsort(target_device, stable=True)
    outgoing = stacked[send_order].reshape(device_count, peer_rows, 3, head_width)
    local_slot = (packed_index % row_count)[send_order].reshape(device_count, peer_rows)
    incoming, incoming_slot = (
        lax.all_to_all(outgoing, "fsdp", split_axis=0, concat_axis=0, tiled=True),
        lax.all_to_all(local_slot, "fsdp", split_axis=0, concat_axis=0, tiled=True),
    )
    incoming_slot = incoming_slot.reshape(row_count)
    packed = incoming.reshape(row_count, 3, head_width)[jnp.argsort(incoming_slot)]
    unit_blocks = packed.reshape(row_count, 3, 8, unit_width).transpose(2, 0, 1, 3)
    unit_blocks = unit_blocks.reshape(2, 2, 2, row_count, 3, unit_width)
    is_wide = group_size == 8
    group_rank = device - group_start

    def forward_swap(sending, bit_number):
        return partner(sending, "fsdp", bit_number)

    def backward_swap(sending, bit_number):
        return partner(sending, "fsdp", bit_number)

    unit_blocks = butterfly(unit_blocks, group_rank, is_wide, forward_swap)
    attended = attend(unit_blocks.reshape(8 * row_count, 3, unit_width), labels, unit_heads)
    results = butterfly(
        attended.reshape(2, 2, 2, row_count, unit_width), group_rank, is_wide, backward_swap
    )
    packed_out = (
        results.reshape(8, row_count, unit_width).transpose(1, 0, 2).reshape(row_count, head_width)
    )
    mixed_packed = jnp.dot(
        packed_out,
        lax.all_gather(out_weight, "fsdp", axis=0, tiled=True),
        preferred_element_type=jnp.float32,
    ).astype(jnp.bfloat16)
    returning = mixed_packed[incoming_slot].reshape(device_count, peer_rows, mixed_packed.shape[1])
    returned = lax.all_to_all(returning, "fsdp", split_axis=0, concat_axis=0, tiled=True).reshape(
        row_count, mixed_packed.shape[1]
    )
    return returned[jnp.argsort(send_order)]


def solution(mesh):
    placed = (
        P(("dp", "fsdp"), None, None),
        P(None, ("dp", "fsdp")),
        P(("dp", "fsdp")),
        P("dp"),
        P("dp"),
        P(),
        P(),
        P("fsdp", None),
    )
    return jax.shard_map(
        on_device, mesh=mesh, in_specs=placed, out_specs=P(("dp", "fsdp"), None), check_vma=False
    )
```

profile of v0, /device:TPU:1, one launch (start us, length us, event | category | flops | bytes accessed | tf_op | source)
XLA Modules:
  0.0 340.2 jit_solution(10470023899819827844)
XLA Ops:
  7.2 2.5 sort.48
  11.7 16.8 %all-to-all-start.1 = ((s32[32,1,4]{2,1,0:T(1,128)}), s32[32,1,4]{2,1,0:T(1,128)S(1)}, u32[]{:S(2)}, u32[]{:S(2)}) async-start(s32[32,1,4]{2,1,0:T(1,128)} %bitcast.18), calls=%async_computation.1 | async-start | bytes 32768 | tf_op jit(solution)/shard_map/all_to_all | solution.py:154
  28.5 2.6 slice_convert_fusion.1
  42.5 2.5 copy.181
  53.8 3.3 add_convert_fusion.1
  58.7 3.6 %gather_fusion.3 = bf16[128,3,2048]{2,1,0:T(4,128)(2,1)} fusion(bf16[128,3,2048]{2,1,0:T(4,128)(2,1)S(1)} %copy.189, s32[1024]{0:T(1024)S(1)} %pad_clamp_fusion.3), kind=kCustom, calls=%fused_computation.3 | custom fusion | bytes 3146240 | tf_op jit(solution)/shard_map/gather | solution.py:150
  62.2 4.6 %copy.190 = bf16[32,4,3,2048]{3,1,2,0:T(4,128)(2,1)} copy(bf16[32,4,3,2048]{3,2,1,0:T(4,128)(2,1)} %bitcast.204) | data formatting | bytes 3145728 | tf_op jit(solution)/shard_map/reshape | solution.py:150
  66.8 12.2 %all-to-all-start = ((bf16[32,4,3,2048]{3,1,2,0:T(4,128)(2,1)}), bf16[32,4,3,2048]{3,1,2,0:T(4,128)(2,1)}, u32[]{:S(2)}, u32[]{:S(2)}) async-start(bf16[32,4,3,2048]{3,1,2,0:T(4,128)(2,1)} %copy.190), calls=%async_computation | async-start | bytes 3145728 | tf_op jit(solution)/shard_map/all_to_all | solution.py:153
  81.2 2.5 sort.49
  83.7 85.9 %all-to-all-done = bf16[32,4,3,2048]{3,1,2,0:T(4,128)(2,1)} async-done(((bf16[32,4,3,2048]{3,1,2,0:T(4,128)(2,1)}), bf16[32,4,3,2048]{3,1,2,0:T(4,128)(2,1)}, u32[]{:S(2)}, u32[]{:S(2)}) %all-to-all-start) | async-done | bytes 1572896 | tf_op jit(solution)/shard_map/all_to_all | solution.py:153
  169.6 2.9 copy.191
  172.5 3.5 %gather_fusion.5 = bf16[128,3,2048]{2,1,0:T(4,128)(2,1)} fusion(bf16[128,3,2048]{2,1,0:T(4,128)(2,1)S(1)} %bitcast.205, s32[1024]{0:T(1024)S(1)} %pad_clamp_fusion.2), kind=kCustom, calls=%fused_computation.5 | custom fusion | bytes 3146240 | tf_op jit(solution)/shard_map/gather | solution.py:157
  176.1 3.2 copy.193
  182.4 2.7 collective-permute-start
  190.9 20.5 %collective-permute-done.1 = bf16[2,2,128,3,256]{4,2,3,0,1:T(8,128)(2,1)} collective-permute-done((bf16[2,2,128,3,256]{4,2,3,0,1:T(8,128)(2,1)S(1)}, bf16[2,2,128,3,256]{4,2,3,0,1:T(8,128)(2,1)}, u32[]{:S(2)}, u32[]{:S(2)}) %collective-permute-start.1) | collective-permute-done | bytes 786464 | tf_op jit(solution)/shard_map/ppermute | solution.py:18
  215.3 36.0 %collective-permute-done.2 = bf16[2,2,128,3,256]{4,2,3,1,0:T(8,128)(2,1)S(1)} collective-permute-done((bf16[2,2,128,3,256]{4,2,3,1,0:T(8,128)(2,1)S(1)}, bf16[2,2,128,3,256]{4,2,3,1,0:T(8,128)(2,1)S(1)}, u32[]{:S(2)}, u32[]{:S(2)}) %collective-permute-start.2) | collective-permute-done | bytes 786464 | tf_op jit(solution)/shard_map/ppermute | solution.py:18
  252.8 9.3 %while.22 = (s32[]{:T(128)}, bf16[2,512,256]{2,1,0:T(8,128)(2,1)S(1)}, s32[2]{0:T(128)S(1)}, s32[1024]{0:T(1024)S(1)}, bf16[1024,2,128]{0,2,1:T(8,128)(2,1)S(1)}...) while((s32[]{:T(128)}, ...), condition=%wide.region_8.15_spmd, body=%wide.region_6.14_spmd.sunk | while | flops 544865280 | bytes 12601523 | solution.py:125
  262.2 2.4 collective-permute-start.3
  267.9 7.4 %collective-permute-done.4 = bf16[2,2,128,256]{3,2,0,1:T(8,128)(2,1)S(1)} collective-permute-done((bf16[2,2,128,256]{3,2,0,1:T(8,128)(2,1)S(1)}, bf16[2,2,128,256]{3,2,0,1:T(8,128)(2,1)S(1)}, u32[]{:S(2)}, u32[]{:S(2)}) %collective-permute-start.4) | collective-permute-done | bytes 262176 | tf_op jit(solution)/shard_map/ppermute | solution.py:18
  277.5 14.4 %collective-permute-done.5 = bf16[2,2,128,256]{3,2,1,0:T(8,128)(2,1)S(1)} collective-permute-done((bf16[2,2,128,256]{3,2,1,0:T(8,128)(2,1)S(1)}, bf16[2,2,128,256]{3,2,1,0:T(8,128)(2,1)S(1)}, u32[]{:S(2)}, u32[]{:S(2)}) %collective-permute-start.5) | collective-permute-done | bytes 262176 | tf_op jit(solution)/shard_map/ppermute | solution.py:18
  292.4 3.8 %convolution_convert_fusion = bf16[128,1536]{1,0:T(8,128)(2,1)S(1)} fusion(bf16[128,2048]{0,1:T(8,128)(2,1)S(1)} %bitcast.218, bf16[2048,1536]{1,0:T(8,128)(2,1)} %all-gather.2.cloned.1.call-done), kind=kOutput, calls=%fused_computation.20 | convolution fusion | flops 805502976 | bytes 7208960 | tf_op jit(solution)/shard_map/dot_general | solution.py:177
  298.0 5.6 %all-to-all-start.2 = ((bf16[32,4,1536]{2,1,0:T(4,128)(2,1)}), bf16[32,4,1536]{2,1,0:T(4,128)(2,1)S(1)}, u32[]{:S(2)}, u32[]{:S(2)}) async-start(bf16[32,4,1536]{2,1,0:T(4,128)(2,1)} %reshape.293), calls=%async_computation.2 | async-start | bytes 786432 | tf_op jit(solution)/shard_map/all_to_all | solution.py:183
  303.6 2.6 sort.50
  306.3 25.3 %all-to-all-done.2 = bf16[32,4,1536]{2,1,0:T(4,128)(2,1)S(1)} async-done(((bf16[32,4,1536]{2,1,0:T(4,128)(2,1)}), bf16[32,4,1536]{2,1,0:T(4,128)(2,1)S(1)}, u32[]{:S(2)}, u32[]{:S(2)}) %all-to-all-start.2) | async-done | bytes 393248 | tf_op jit(solution)/shard_map/all_to_all | solution.py:183
  (133 shorter events, 57.8 us)
Async XLA Ops:
  11.7 55.2 %all-to-all-start.1 = ((s32[32,1,4]{2,1,0:T(1,128)}), s32[32,1,4]{2,1,0:T(1,128)S(1)}, u32[]{:S(2)}, u32[]{:S(2)}) async-start(s32[32,1,4]{2,1,0:T(1,128)} %bitcast.18), calls=%async_computation.1 | async-start | bytes 32768 | tf_op jit(solution)/shard_map/all_to_all | solution.py:154
  31.0 0.7 copy-start.8
  31.0 0.7 copy-start.3
  36.0 1.7 copy-start.2
  46.5 1.4 copy-start.7
  46.5 1.4 copy-start.4
  46.5 2.1 copy-start.5
  50.3 3.6 %copy-start.6 = (f32[128]{0:T(128)S(1)}, f32[128]{0:T(128)}, u32[]{:S(2)}) copy-start(f32[128]{0:T(128)} %constant.300.clone) | copy-start | bytes 1540
  50.3 3.6 %copy-start.1 = (bf16[128,3,2048]{2,0,1:T(8,128)(2,1)S(1)}, bf16[128,3,2048]{2,0,1:T(8,128)(2,1)}, u32[]{:S(2)}) copy-start(bf16[128,3,2048]{2,0,1:T(8,128)(2,1)} %param.41) | copy-start | bytes 4718596
  66.8 102.7 %all-to-all-start = ((bf16[32,4,3,2048]{3,1,2,0:T(4,128)(2,1)}), bf16[32,4,3,2048]{3,1,2,0:T(4,128)(2,1)}, u32[]{:S(2)}, u32[]{:S(2)}) async-start(bf16[32,4,3,2048]{3,1,2,0:T(4,128)(2,1)} %copy.190), calls=%async_computation | async-start | bytes 3145728 | tf_op jit(solution)/shard_map/all_to_all | solution.py:153
  79.1 213.4 %all-gather.2.cloned.1.call-start = ((), (), s32[]{:S(2)}) async-start(), calls=%async_computation.3 | async-start | bytes 6488064 | tf_op jit(solution)/shard_map/all_gather | solution.py:179
  180.9 1.4 copy-start
  182.4 4.7 %collective-permute-start = (bf16[2,2,128,3,256]{4,2,3,1,0:T(8,128)(2,1)S(1)}, bf16[2,2,128,3,256]{4,2,3,1,0:T(8,128)(2,1)}, u32[]{:S(2)}, u32[]{:S(2)}) collective-permute-start(bf16[2,2,128,3,256]{4,2,3,1,0:T(8,128)(2,1)S(1)} %bitcast_select_fusion), channel_id=1, source_target_pairs={{0,1},{1,0},{2,3},{3,2},{4,5},{5,4},{6,7},{7,6},{8,9},{9,8},{10,11... | collective-permute-start | bytes 2359304 | tf_op jit(solution)/shard_map/ppermute | solution.py:18
  188.7 2.2 copy-start.9
  188.8 22.6 %collective-permute-start.1 = (bf16[2,2,128,3,256]{4,2,3,0,1:T(8,128)(2,1)S(1)}, bf16[2,2,128,3,256]{4,2,3,0,1:T(8,128)(2,1)}, u32[]{:S(2)}, u32[]{:S(2)}) collective-permute-start(bf16[2,2,128,3,256]{4,2,3,0,1:T(8,128)(2,1)S(1)} %broadcast_select_fusion), channel_id=1, source_target_pairs={{0,2},{1,3},{2,0},{3,1},{4,6},{5,7},{6,4},{7,5},{8,10},{9,11},{10,... | collective-permute-start | bytes 2359304 | tf_op jit(solution)/shard_map/ppermute | solution.py:18
  212.7 2.2 copy-start.10
  212.8 38.4 %collective-permute-start.2 = (bf16[2,2,128,3,256]{4,2,3,1,0:T(8,128)(2,1)S(1)}, bf16[2,2,128,3,256]{4,2,3,1,0:T(8,128)(2,1)S(1)}, u32[]{:S(2)}, u32[]{:S(2)}) collective-permute-start(bf16[2,2,128,3,256]{4,2,3,1,0:T(8,128)(2,1)S(1)} %broadcast_select_fusion.2), channel_id=1, source_target_pairs={{0,4},{1,5},{2,6},{3,7},{4,0},{5,1},{6,2},{7,3},{8,12},{9,13},{10,... | collective-permute-start | bytes 2359304 | tf_op jit(solution)/shard_map/ppermute | solution.py:18
  262.2 3.6 %collective-permute-start.3 = (bf16[2,2,128,256]{3,2,1,0:T(8,128)(2,1)S(1)}, bf16[2,2,128,256]{3,2,1,0:T(8,128)(2,1)S(1)}, u32[]{:S(2)}, u32[]{:S(2)}) collective-permute-start(bf16[2,2,128,256]{3,2,1,0:T(8,128)(2,1)S(1)} %broadcast_select_fusion.4), channel_id=1, source_target_pairs={{0,1},{1,0},{2,3},{3,2},{4,5},{5,4},{6,7},{7,6},{8,9},{9,8},{10,11... | collective-permute-start | bytes 786440 | tf_op jit(solution)/shard_map/ppermute | solution.py:18
  265.8 9.4 %collective-permute-start.4 = (bf16[2,2,128,256]{3,2,0,1:T(8,128)(2,1)S(1)}, bf16[2,2,128,256]{3,2,0,1:T(8,128)(2,1)S(1)}, u32[]{:S(2)}, u32[]{:S(2)}) collective-permute-start(bf16[2,2,128,256]{3,2,0,1:T(8,128)(2,1)S(1)} %broadcast_select_fusion.6), channel_id=1, source_target_pairs={{0,2},{1,3},{2,0},{3,1},{4,6},{5,7},{6,4},{7,5},{8,10},{9,11},{10,... | collective-permute-start | bytes 786440 | tf_op jit(solution)/shard_map/ppermute | solution.py:18
  275.4 16.6 %collective-permute-start.5 = (bf16[2,2,128,256]{3,2,1,0:T(8,128)(2,1)S(1)}, bf16[2,2,128,256]{3,2,1,0:T(8,128)(2,1)S(1)}, u32[]{:S(2)}, u32[]{:S(2)}) collective-permute-start(bf16[2,2,128,256]{3,2,1,0:T(8,128)(2,1)S(1)} %broadcast_select_fusion.8), channel_id=1, source_target_pairs={{0,4},{1,5},{2,6},{3,7},{4,0},{5,1},{6,2},{7,3},{8,12},{9,13},{10,... | collective-permute-start | bytes 786440 | tf_op jit(solution)/shard_map/ppermute | solution.py:18
  298.0 33.6 %all-to-all-start.2 = ((bf16[32,4,1536]{2,1,0:T(4,128)(2,1)}), bf16[32,4,1536]{2,1,0:T(4,128)(2,1)S(1)}, u32[]{:S(2)}, u32[]{:S(2)}) async-start(bf16[32,4,1536]{2,1,0:T(4,128)(2,1)} %reshape.293), calls=%async_computation.2 | async-start | bytes 786432 | tf_op jit(solution)/shard_map/all_to_all | solution.py:183
Sparse Core Ops, SparseCore 0:
  82.0 118.7 all-gather.1
where the time goes:
time: 341 us; the launch traced here: 340 us
  waiting for transfers between devices  193 us (57%)
  local copies, waits for them, and re-layouts  51.4 us (15%)
  starting transfers between devices  47.7 us (14%)
  other arithmetic  23 us (7%)
  between operations  14.1 us (4%)
  matrix products  9.44 us (3%)
    all_to_all x1, waiting for transfers between devices, on_device(): lax.all_to_all(outgoing, 'fsdp', split_axis=0, concat_axis=0, tiled=True)  85.9 us
    ppermute x6, waiting for transfers between devices, partner(): lax.ppermute(value, axis, [(i, i ^ 1 << apart) for i in range(lax.axis_si...  81.4 us
    all_to_all x1, waiting for transfers between devices, on_device(): lax.all_to_all(returning, 'fsdp', split_axis=0, concat_axis=0, tiled=True)  25.3 us
    all_to_all x1, starting transfers between devices, on_device(): lax.all_to_all(local_slot, 'fsdp', split_axis=0, concat_axis=0, tiled=True)  16.8 us
    ppermute x6, starting transfers between devices, partner(): lax.ppermute(value, axis, [(i, i ^ 1 << apart) for i in range(lax.axis_si...  13 us
    all_to_all x1, starting transfers between devices, on_device(): lax.all_to_all(outgoing, 'fsdp', split_axis=0, concat_axis=0, tiled=True)  12.2 us
    gather x6, local copies, waits for them, and re-layouts, normed(): entries[..., partner_table] * sign_table * sine_part  9.44 us
  transfers between devices with their start and end apart: 10, of which 8 were waited for; matrix products, arithmetic and copies ran while one was open for 21% of the time, Pallas kernels for 0%

commit v1 on v0

v1 whole, which is shorter than its diff:
```python
import functools
import math

import jax
import jax.numpy as jnp
import numpy as np
from jax import lax
from jax.experimental import pallas as pl
from jax.experimental.pallas import tpu as pltpu
from jax.sharding import PartitionSpec as P

MESH = pl.DeviceIdType.MESH
HD = 128
CLIPS = 24
GROUPS = 6
ROPE_BASE = 256.0
NORM_EPS = 1e-06
MASKED = -30000.0
BF16 = jnp.bfloat16
F32 = jnp.float32


def rope_rows():
    table = np.zeros((8, HD), np.float32)
    lead = HD // 8
    side = (HD - lead) // 2
    offset = 0
    for section in (lead, side, side):
        middle = section // 2
        for column in range(section):
            within = column % middle
            table[0, offset + column] = ROPE_BASE ** (-2.0 * within / section)
            first = column < middle
            table[1, offset + column] = -1.0 if first else 1.0
            table[2, offset + column] = offset + column + (middle if first else -middle)
        offset += section
    return table


def group_base(group):
    return 1024 * group if group < 2 else 2048 + 512 * (group - 2)


def kernel(
    n_dp, q_parts, c_parts,
    x_ref, pos_ref, idx_ref, len_ref, grp_ref, qg_ref, kg_ref, w_ref, tab_ref,
    out_ref,
    send, recv, lab_send, lab_recv, osend, orecv, wfull, hot_q, hot_k, perm, acc,
    send_sem, recv_sem, lab_sems, ret_send, ret_recv, own_sem,
    wz_sems, xy_send, xy_recv, sib_sems,
):
    n = 32
    dp = lax.axis_index("dp")
    me = lax.axis_index("fsdp")
    core = me % 2
    chip = me // 2
    sibling = me + 1 - 2 * core
    q_part = dp // c_parts
    c_part = dp % c_parts
    w_rows, w_cols = 64 // q_parts, 1536 // c_parts

    def slot_of(row, side):
        return (row % c_parts) * (2 * q_parts) + side * q_parts + row // c_parts

    def far_first(step):
        near = n - 1 - step
        return (me + jnp.where(near % 2 == 1, (near + 1) // 2, n - near // 2)) % n

    barrier = pltpu.get_barrier_semaphore()

    @pl.loop(1, n)
    def _(i):
        pl.semaphore_signal(barrier, inc=1, device_id={"fsdp": (me + i) % n}, device_id_type=MESH)

    if n_dp > 1:
        @pl.loop(1, n_dp)
        def _(i):
            pl.semaphore_signal(barrier, inc=1, device_id={"dp": (dp + i) % n_dp}, device_id_type=MESH)

    idx = idx_ref[...].astype(F32)
    across = jnp.broadcast_to(idx, (HD, HD))
    down = across.T
    rank = jnp.sum((down < across).astype(F32), axis=0, keepdims=True)
    row_id = lax.broadcasted_iota(jnp.int32, (HD, HD), 0).astype(F32)
    lane_id = lax.broadcasted_iota(jnp.int32, (HD, HD), 1).astype(F32)
    rank_rows = jnp.broadcast_to(rank, (HD, HD))
    to_sorted = (rank_rows == row_id).astype(F32).astype(BF16)
    perm[...] = (rank_rows.T == lane_id).astype(F32).astype(BF16)

    running = [jnp.int32(group_base(g)) for g in range(GROUPS)]
    label = jnp.zeros((1, HD), F32)
    for clip in range(CLIPS):
        length, group = len_ref[clip], grp_ref[clip]
        end = jnp.int32(0)
        for g in range(GROUPS):
            inside = group == g
            running[g] = running[g] + jnp.where(inside, length, 0)
            end = end + jnp.where(inside, running[g], 0)
        label = label + (idx_ref[...] >= end).astype(F32)
    ordered = lax.dot_general(
        jnp.broadcast_to(label, (8, HD)).astype(BF16), to_sorted,
        (((1,), (1,)), ((), ())), preferred_element_type=F32,
    )
    lane = lax.broadcasted_iota(jnp.int32, (8, HD), 1)
    window = 32 * (me % 4)
    for g in range(GROUPS):
        if g < 2:
            shown = pltpu.roll(ordered, (window - 32 * g + HD) % HD, 1)
        else:
            first = 64 + 16 * (g - 2)
            low = pltpu.roll(ordered, (window - first + HD) % HD, 1)
            high = pltpu.roll(ordered, (window + 16 - first + HD) % HD, 1) + 32.0
            shown = jnp.where(lane >= window + 16, high, low)
        shown = jnp.where((lane >= window) & (lane < window + 32), shown, 0.0)
        lab_send[g] = shown[0:1]

    freq = tab_ref[0:1, :]
    sign = tab_ref[1:2, :]
    swap = (jnp.broadcast_to(tab_ref[2:3, :], (HD, HD)) == row_id).astype(F32)
    pos = pos_ref[...].astype(F32)
    section = jnp.where(
        row_id < 16, pos[0:1, :], jnp.where(row_id < 72, pos[1:2, :], pos[2:3, :])
    ).astype(BF16)
    place = lax.dot_general(
        to_sorted, section, (((1,), (1,)), ((), ())), preferred_element_type=F32
    )
    angles = place * freq
    cosine = jnp.cos(angles)
    sine = jnp.sin(angles) * sign
    swap_b = swap.astype(BF16)
    tables = []
    for gain_ref in (qg_ref, kg_ref):
        gain = gain_ref[...]
        gain_down = jnp.broadcast_to(gain, (HD, HD)).T
        turned = jnp.sum(gain_down * swap, axis=0, keepdims=True)
        tables.append((cosine * gain, sine * turned))

    pl.semaphore_wait(barrier, n - 1 + (n_dp - 1))

    def w_mine():
        return w_ref.at[
            pl.ds(pl.multiple_of(q_part * w_rows, w_rows), w_rows),
            pl.ds(pl.multiple_of(c_part * w_cols, w_cols), w_cols),
        ]

    my_slot = slot_of(dp, core)
    w_place = wfull.at[chip // 2, chip % 2, my_slot]
    w_own = pltpu.make_async_copy(w_mine(), w_place, own_sem.at[0])
    w_own.start()

    @pl.loop(1, 16)
    def _(i):
        pltpu.make_async_remote_copy(
            src_ref=w_mine(), dst_ref=w_place, send_sem=wz_sems.at[0], recv_sem=wz_sems.at[1],
            device_id={"fsdp": 2 * ((chip + i) % 16) + core}, device_id_type=MESH,
        ).start()

    def group_of(peer):
        return jnp.where(peer < 16, peer // 8, 2 + (peer - 16) // 4)

    @pl.loop(0, n - 1)
    def _(i):
        peer = far_first(i)
        pltpu.make_async_remote_copy(
            src_ref=lab_send.at[group_of(peer)], dst_ref=lab_recv.at[me],
            send_sem=lab_sems.at[0], recv_sem=lab_sems.at[1],
            device_id={"fsdp": peer}, device_id_type=MESH,
        ).start()

    lab_own = pltpu.make_async_copy(lab_send.at[group_of(me)], lab_recv.at[me], own_sem.at[1])
    lab_own.start()

    def prepare(half):
        def one(m, carry):
            columns = pl.ds(pl.multiple_of((2 * m + half) * HD, HD), HD)
            for kind in range(3):
                entries = jnp.dot(to_sorted, x_ref[kind, :, columns], preferred_element_type=F32)
                if kind < 2:
                    cos_gain, sin_gain = tables[kind]
                    swapped = jnp.dot(entries.astype(BF16), swap_b, preferred_element_type=F32)
                    mean = jnp.sum(entries * entries, axis=1, keepdims=True) * (1.0 / HD)
                    factor = lax.rsqrt(mean + NORM_EPS)
                    entries = (entries * cos_gain + swapped * sin_gain) * factor
                rows = entries.astype(BF16)
                for g in range(2):
                    send[half, 8 * g + m, kind] = rows[32 * g:32 * g + 32]
                for g in range(4):
                    send[half, 16 + 4 * g + m // 2, kind, pl.ds(pl.multiple_of(16 * (m % 2), 16), 16)] = (
                        rows[64 + 16 * g:80 + 16 * g]
                    )
            return carry

        lax.fori_loop(0, 8, one, 0)

        @pl.loop(0, n - 1)
        def _(i):
            peer = far_first(i)
            pltpu.make_async_remote_copy(
                src_ref=send.at[half, peer], dst_ref=recv.at[half, me],
                send_sem=send_sem.at[half], recv_sem=recv_sem.at[half],
                device_id={"fsdp": peer}, device_id_type=MESH,
            ).start()

        copy = pltpu.make_async_copy(send.at[half, me], recv.at[half, me], own_sem.at[2 + half])
        copy.start()
        return copy

    own_first = prepare(0)

    def ring_total():
        return wfull.at[:, :, 0]

    def ring_wait():
        view = wfull.at[pl.ds(0, 5), pl.ds(0, 1), pl.ds(0, 3)]
        return pltpu.make_async_remote_copy(
            src_ref=view, dst_ref=view, send_sem=wz_sems.at[0], recv_sem=wz_sems.at[1],
            device_id={"fsdp": sibling}, device_id_type=MESH,
        )

    w_own.wait()
    if q_parts * c_parts > 1:
        ring_wait().wait_recv()
    else:
        @pl.loop(1, 16)
        def _(i):
            pltpu.make_async_remote_copy(
                src_ref=w_mine(), dst_ref=w_place, send_sem=wz_sems.at[0], recv_sem=wz_sems.at[1],
                device_id={"fsdp": sibling}, device_id_type=MESH,
            ).wait_recv()

    def xy_copy(to, source):
        part = wfull.at[:, :, slot_of(source, core)]
        return pltpu.make_async_remote_copy(
            src_ref=part, dst_ref=part, send_sem=xy_send, recv_sem=xy_recv.at[source],
            device_id={"dp": to}, device_id_type=MESH,
        )

    if n_dp > 1:
        @pl.loop(1, n_dp)
        def _(i):
            xy_copy((dp + i) % n_dp, dp).start()

    def sib_copy(source):
        part = wfull.at[:, :, slot_of(source, core)]
        return pltpu.make_async_remote_copy(
            src_ref=part, dst_ref=part, send_sem=sib_sems.at[0], recv_sem=sib_sems.at[1],
            device_id={"fsdp": sibling}, device_id_type=MESH,
        )

    sib_copy(dp).start()

    own_second = prepare(1)

    def label_wait():
        view = lab_recv.at[pl.ds(0, n - 1)]
        return pltpu.make_async_remote_copy(
            src_ref=view, dst_ref=view, send_sem=lab_sems.at[0], recv_sem=lab_sems.at[1],
            device_id={"fsdp": sibling}, device_id_type=MESH,
        )

    lab_own.wait()
    label_wait().wait_recv()
    for block in range(8):
        row = lab_recv[4 * block] + lab_recv[4 * block + 1] + lab_recv[4 * block + 2] + lab_recv[4 * block + 3]
        same = jnp.broadcast_to(row, (HD, HD)).T == lane_id
        hot_q[block * HD:(block + 1) * HD] = jnp.where(same, 1.0, 0.0).astype(BF16)
        hot_k[block * HD:(block + 1) * HD] = jnp.where(same, 0.0, MASKED).astype(BF16)

    def half_wait(half):
        view = recv.at[half, pl.ds(0, n - 1)]
        return pltpu.make_async_remote_copy(
            src_ref=view, dst_ref=view, send_sem=send_sem.at[half], recv_sem=recv_sem.at[half],
            device_id={"fsdp": sibling}, device_id_type=MESH,
        )

    def back_wait(half):
        view = orecv.at[half, pl.ds(0, n - 1)]
        return pltpu.make_async_remote_copy(
            src_ref=view, dst_ref=view, send_sem=ret_send.at[half], recv_sem=ret_recv.at[half],
            device_id={"fsdp": sibling}, device_id_type=MESH,
        )

    scale = math.log2(math.e) / math.sqrt(HD)

    def attend(half, own_copy):
        own_copy.wait()
        half_wait(half).wait_recv()

        def block(step, carry):
            turn = jnp.where(step == 0, 2, jnp.where(step == 1, 1, jnp.where(step == 2, 3, 0)))
            part = (me // 8 + turn) % 4
            first = pl.multiple_of(8 * part, 8)
            queries = jnp.concatenate(
                [recv[half, pl.ds(first, 8), 0].reshape(256, HD),
                 hot_q[pl.ds(pl.multiple_of(256 * part, 256), 256)]], axis=1)
            total = jnp.zeros((256, 2 * HD), F32)
            for key_part in range(4):
                keys = jnp.concatenate(
                    [recv[half, 8 * key_part:8 * key_part + 8, 1].reshape(256, HD),
                     hot_k[256 * key_part:256 * key_part + 256]], axis=1)
                values = jnp.concatenate(
                    [recv[half, 8 * key_part:8 * key_part + 8, 2].reshape(256, HD),
                     jnp.ones((256, HD), BF16)], axis=1)
                scores = lax.dot_general(
                    queries, keys, (((1,), (1,)), ((), ())), preferred_element_type=F32)
                weights = jnp.exp2(scores * scale).astype(BF16)
                total = total + jnp.dot(weights, values, preferred_element_type=F32)
            result = (total[:, :HD] / total[:, HD:]).astype(BF16)
            osend[half, pl.ds(first, 8)] = result.reshape(8, 32, HD)

            @pl.loop(0, 8)
            def _(i):
                peer = first + (me + i) % 8

                @pl.when(peer != me)
                def _():
                    pltpu.make_async_remote_copy(
                        src_ref=osend.at[half, peer], dst_ref=orecv.at[half, me],
                        send_sem=ret_send.at[half], recv_sem=ret_recv.at[half],
                        device_id={"fsdp": peer}, device_id_type=MESH,
                    ).start()
            return carry

        lax.fori_loop(0, 4, block, 0)
        copy = pltpu.make_async_copy(osend.at[half, me], orecv.at[half, me], own_sem.at[4 + half])
        copy.start()
        return copy

    back_first = attend(0, own_first)

    if n_dp > 1:
        @pl.loop(1, n_dp)
        def _(i):
            source = (dp + n_dp - i) % n_dp
            xy_copy(dp, source).wait_recv()
            sib_copy(source).start()

    back_second = attend(1, own_second)

    def sib_wait():
        view = wfull.at[:, :, pl.ds(0, n_dp)]
        return pltpu.make_async_remote_copy(
            src_ref=view, dst_ref=view, send_sem=sib_sems.at[0], recv_sem=sib_sems.at[1],
            device_id={"fsdp": sibling}, device_id_type=MESH,
        )

    sib_wait().wait_recv()

    def gathered(half):
        heads = []
        for m in range(8):
            parts = [orecv[half, m], orecv[half, 8 + m]]
            for g in range(4):
                parts.append(orecv[half, 16 + 4 * g + m // 2, 16 * (m % 2):16 * (m % 2) + 16])
            heads.append(jnp.concatenate(parts, axis=0))
        return jnp.concatenate(heads, axis=1)

    def project(half, c):
        rows = wfull[:, half, 2 * q_parts * c:2 * q_parts * (c + 1)].reshape(8 * HD, w_cols)
        return rows

    back_first.wait()
    back_wait(0).wait_recv()
    left = gathered(0)
    for c in range(c_parts):
        acc[:, c * w_cols:(c + 1) * w_cols] = jnp.dot(left, project(0, c), preferred_element_type=F32)
    back_second.wait()
    back_wait(1).wait_recv()
    left = gathered(1)
    for c in range(c_parts):
        columns = slice(c * w_cols, (c + 1) * w_cols)
        mixed = acc[:, columns] + jnp.dot(left, project(1, c), preferred_element_type=F32)
        out_ref[:, columns] = jnp.dot(
            perm[...], mixed.astype(BF16), preferred_element_type=F32
        ).astype(BF16)

    for half in range(2):
        half_wait(half).wait_send()
        back_wait(half).wait_send()
    label_wait().wait_send()
    if q_parts * c_parts > 1:
        ring_wait().wait_send()
    else:
        @pl.loop(1, 16)
        def _(i):
            pltpu.make_async_remote_copy(
                src_ref=w_mine(), dst_ref=w_place, send_sem=wz_sems.at[0], recv_sem=wz_sems.at[1],
                device_id={"fsdp": sibling}, device_id_type=MESH,
            ).wait_send()
    if n_dp > 1:
        view = wfull.at[:, :, pl.ds(0, n_dp - 1)]
        pltpu.make_async_remote_copy(
            src_ref=view, dst_ref=view, send_sem=xy_send, recv_sem=xy_recv.at[0],
            device_id={"fsdp": sibling}, device_id_type=MESH,
        ).wait_send()
    sib_wait().wait_send()


def on_device(n_dp, projections, positions, packed_index, clip_length, clip_group, query_gain, key_gain, out_weight):
    q_parts, c_parts = {16: (4, 4), 2: (1, 2), 1: (1, 1)}[n_dp]
    vmem = pl.BlockSpec(memory_space=pltpu.VMEM)
    smem = pl.BlockSpec(memory_space=pltpu.SMEM)
    dma = pltpu.SemaphoreType.DMA
    return pl.pallas_call(
        functools.partial(kernel, n_dp, q_parts, c_parts),
        out_shape=jax.ShapeDtypeStruct((128, 1536), BF16),
        in_specs=[vmem, vmem, vmem, smem, smem, vmem, vmem, vmem, vmem],
        out_specs=vmem,
        scratch_shapes=[
            pltpu.VMEM((2, 32, 3, 32, HD), BF16),
            pltpu.VMEM((2, 32, 3, 32, HD), BF16),
            pltpu.VMEM((GROUPS, 1, HD), F32),
            pltpu.VMEM((32, 1, HD), F32),
            pltpu.VMEM((2, 32, 32, HD), BF16),
            pltpu.VMEM((2, 32, 32, HD), BF16),
            pltpu.VMEM((8, 2, 2 * q_parts * c_parts, 64 // q_parts, 1536 // c_parts), BF16),
            pltpu.VMEM((8 * HD, HD), BF16),
            pltpu.VMEM((8 * HD, HD), BF16),
            pltpu.VMEM((HD, HD), BF16),
            pltpu.VMEM((HD, 1536), F32),
            dma((2,)),
            dma((2,)),
            dma((2,)),
            dma((2,)),
            dma((2,)),
            dma((6,)),
            dma((2,)),
            dma,
            dma((n_dp,)),
            dma((2,)),
        ],
        compiler_params=pltpu.CompilerParams(
            collective_id=0, has_side_effects=True, vmem_limit_bytes=40 * 1024 * 1024
        ),
        cost_estimate=pl.CostEstimate(flops=3_500_000_000, bytes_accessed=4_000_000, transcendentals=2_500_000),
    )(
        projections.transpose(1, 0, 2),
        positions,
        packed_index.reshape(1, 128),
        clip_length,
        clip_group,
        query_gain.reshape(1, HD),
        key_gain.reshape(1, HD),
        out_weight,
        jnp.asarray(rope_rows()),
    )


def solution(mesh):
    placed = (
        P(("dp", "fsdp"), None, None),
        P(None, ("dp", "fsdp")),
        P(("dp", "fsdp")),
        P("dp"),
        P("dp"),
        P(),
        P(),
        P("fsdp", None),
    )
    return jax.shard_map(
        functools.partial(on_device, mesh.shape["dp"]),
        mesh=mesh, in_specs=placed, out_specs=P(("dp", "fsdp"), None), check_vma=False,
    )
```

time: 341 us -> 128 us (0.38)
  waiting for transfers between devices: 193 us -> 0 us
  Pallas kernels: 0 us -> 120 us
  starting transfers between devices: 47.7 us -> 0 us
  local copies, waits for them, and re-layouts: 51.4 us -> 7.72 us
  other arithmetic: 23 us -> 0 us
  between operations: 14.1 us -> 0.02 us
  matrix products: 9.44 us -> 0 us
    pallas_call x0 -> x1, Pallas kernels: none -> 120 us  [on_device(): pl.pallas_call(functools.partial(kernel, n_dp, q_parts, c_parts), out_sha...]
    all_to_all x3 -> x0, waiting for transfers between devices: 111 us -> none  [the longest x1 85.9 us: on_device(): lax.all_to_all(outgoing, 'fsdp', split_axis=0, concat_axis=0, tiled=True)]
    ppermute x6 -> x0, waiting for transfers between devices: 81.4 us -> none  [partner(): lax.ppermute(value, axis, [(i, i ^ 1 << apart) for i in range(lax.axis_si...]
    all_to_all x3 -> x0, starting transfers between devices: 34.6 us -> none  [the longest x1 16.8 us: on_device(): lax.all_to_all(local_slot, 'fsdp', split_axis=0, concat_axis=0, tiled=True)]
    gather x13 -> x0, local copies, waits for them, and re-layouts: 24.2 us -> none  [the longest x6 9.44 us: normed(): entries[..., partner_table] * sign_table * sine_part]
    ppermute x6 -> x0, starting transfers between devices: 13 us -> none  [partner(): lax.ppermute(value, axis, [(i, i ^ 1 << apart) for i in range(lax.axis_si...]
    dot_general x5 -> x0, matrix products: 9.44 us -> none  [the longest x1 3.8 us: on_device(): jnp.dot(packed_out, lax.all_gather(out_weight, 'fsdp', axis=0, tiled=True...]
    sort x3 -> x0, other arithmetic: 7.69 us -> none  [the longest x1 2.62 us: on_device(): return returned[jnp.argsort(send_order)]]
  transfers between devices with their start and end apart: 10 -> 0, of which waited for: 8 -> 0; matrix products, arithmetic and copies ran while one was open for 21% -> 0% of each run, Pallas kernels for 0% -> 0%
where the time goes in v1:
time: 128 us
  Pallas kernels  120 us (94%)
  local copies, waits for them, and re-layouts  7.72 us (6%)
    pallas_call x1, Pallas kernels, on_device(): pl.pallas_call(functools.partial(kernel, n_dp, q_parts, c_parts), out_sha...  120 us
    unnamed x19, local copies, waits for them, and re-layouts  7.72 us

profile of v1, /device:TPU:1, one launch (start us, length us, event | category | flops | bytes accessed | tf_op | source)
XLA Modules:
  0.0 127.6 jit_solution(12696254396544539479)
XLA Ops:
  0.0 0.0 copy-start
  0.0 1.4 %copy-done = bf16[128,3,2048]{2,0,1:T(8,128)(2,1)S(1)} copy-done((bf16[128,3,2048]{2,0,1:T(8,128)(2,1)S(1)}, bf16[128,3,2048]{2,0,1:T(8,128)(2,1)}, u32[]{:S(2)}) %copy-start) | copy-done | bytes 1572888
  1.4 0.0 copy-start.1
  1.4 0.9 copy-done.1
  2.3 0.0 copy-start.2
  2.3 0.7 copy-done.2
  3.0 0.0 copy-start.3
  3.0 0.7 copy-done.3
  3.7 0.0 copy-start.4
  3.7 0.7 copy-done.4
  4.3 0.0 copy-start.5
  4.3 0.7 copy-done.5
  5.0 0.0 copy-start.6
  5.0 0.7 copy-done.6
  5.6 0.0 copy-start.7
  5.6 0.7 copy-done.7
  6.3 0.0 copy-start.8
  6.3 0.7 copy-done.8
  7.0 119.9 %shard_map.91 = bf16[128,1536]{1,0:T(8,128)(2,1)S(1)} custom-call(bf16[3,128,2048]{2,1,0:T(8,128)(2,1)S(1)} %bitcast.4, s32[3,128]{1,0:T(4,128)S(1)} %copy-done.2, s32[1,128]{1,0:T(1,128)S(1)} %bitcast.5, s32[24]{0:T(128)S(1)} %copy-done.4, s32[24]{0:T(128)S(1)} %copy-done.5, f32[1,128]{1,0:T(1,128)S(1)} %bitcast.6, f32[1,128]{1,0:T(1,128)S(1)} %bitcast.7, ...), custom_call_target="tpu_custom_call" | custom-call | flops 3500000000 | bytes 4000000 | tf_op jit(solution)/shard_map/pallas_call | solution.py:404
  126.9 0.7 copy.11
Async XLA Ops:
  0.0 1.4 %copy-start = (bf16[128,3,2048]{2,0,1:T(8,128)(2,1)S(1)}, bf16[128,3,2048]{2,0,1:T(8,128)(2,1)}, u32[]{:S(2)}) copy-start(bf16[128,3,2048]{2,0,1:T(8,128)(2,1)} %param.9) | copy-start | bytes 4718596
  1.4 0.9 copy-start.1
  2.3 0.7 copy-start.2
  3.0 0.7 copy-start.3
  3.7 0.7 copy-start.4
  4.3 0.7 copy-start.5
  5.0 0.7 copy-start.6
  5.6 0.7 copy-start.7
  6.3 0.7 copy-start.8

commit v2 on v1

--- a/solution.py
+++ b/solution.py
@@ -43,8 +43,9 @@
 
 def kernel(
     n_dp, q_parts, c_parts,
-    x_ref, pos_ref, idx_ref, len_ref, grp_ref, qg_ref, kg_ref, w_ref, tab_ref,
+    x_hbm, pos_hbm, idx_hbm, len_hbm, grp_hbm, qg_hbm, kg_hbm, w_ref, tab_hbm,
     out_ref,
+    x_ref, pos_ref, idx_ref, len_ref, grp_ref, qg_ref, kg_ref, tab_ref, in_sems,
     send, recv, lab_send, lab_recv, osend, orecv, wfull, hot_q, hot_k, perm, acc,
     send_sem, recv_sem, lab_sems, ret_send, ret_recv, own_sem,
     wz_sems, xy_send, xy_recv, sib_sems,
@@ -77,6 +78,18 @@
         def _(i):
             pl.semaphore_signal(barrier, inc=1, device_id={"dp": (dp + i) % n_dp}, device_id_type=MESH)
 
+    arrivals = [
+        pltpu.make_async_copy(source, target, in_sems.at[i])
+        for i, (source, target) in enumerate((
+            (idx_hbm, idx_ref), (len_hbm, len_ref), (grp_hbm, grp_ref), (pos_hbm, pos_ref),
+            (qg_hbm, qg_ref), (kg_hbm, kg_ref), (tab_hbm, tab_ref), (x_hbm, x_ref),
+        ))
+    ]
+    for arrival in arrivals:
+        arrival.start()
+    for arrival in arrivals[:-1]:
+        arrival.wait()
+
     idx = idx_ref[...].astype(F32)
     across = jnp.broadcast_to(idx, (HD, HD))
     down = across.T
@@ -134,41 +147,6 @@
         gain_down = jnp.broadcast_to(gain, (HD, HD)).T
         turned = jnp.sum(gain_down * swap, axis=0, keepdims=True)
         tables.append((cosine * gain, sine * turned))
-
-    pl.semaphore_wait(barrier, n - 1 + (n_dp - 1))
-
-    def w_mine():
-        return w_ref.at[
-            pl.ds(pl.multiple_of(q_part * w_rows, w_rows), w_rows),
-            pl.ds(pl.multiple_of(c_part * w_cols, w_cols), w_cols),
-        ]
-
-    my_slot = slot_of(dp, core)
-    w_place = wfull.at[chip // 2, chip % 2, my_slot]
-    w_own = pltpu.make_async_copy(w_mine(), w_place, own_sem.at[0])
-    w_own.start()
-
-    @pl.loop(1, 16)
-    def _(i):
-        pltpu.make_async_remote_copy(
-            src_ref=w_mine(), dst_ref=w_place, send_sem=wz_sems.at[0], recv_sem=wz_sems.at[1],
-            device_id={"fsdp": 2 * ((chip + i) % 16) + core}, device_id_type=MESH,
-        ).start()
-
-    def group_of(peer):
-        return jnp.where(peer < 16, peer // 8, 2 + (peer - 16) // 4)
-
-    @pl.loop(0, n - 1)
-    def _(i):
-        peer = far_first(i)
-        pltpu.make_async_remote_copy(
-            src_ref=lab_send.at[group_of(peer)], dst_ref=lab_recv.at[me],
-            send_sem=lab_sems.at[0], recv_sem=lab_sems.at[1],
-            device_id={"fsdp": peer}, device_id_type=MESH,
-        ).start()
-
-    lab_own = pltpu.make_async_copy(lab_send.at[group_of(me)], lab_recv.at[me], own_sem.at[1])
-    lab_own.start()
 
     def prepare(half):
         def one(m, carry):
@@ -192,7 +170,8 @@
 
         lax.fori_loop(0, 8, one, 0)
 
-        @pl.loop(0, n - 1)
+    def send_some(half, first, last):
+        @pl.loop(first, last)
         def _(i):
             peer = far_first(i)
             pltpu.make_async_remote_copy(
@@ -201,35 +180,73 @@
                 device_id={"fsdp": peer}, device_id_type=MESH,
             ).start()
 
+    def keep_own(half):
         copy = pltpu.make_async_copy(send.at[half, me], recv.at[half, me], own_sem.at[2 + half])
         copy.start()
         return copy
 
-    own_first = prepare(0)
-
-    def ring_total():
-        return wfull.at[:, :, 0]
-
-    def ring_wait():
-        view = wfull.at[pl.ds(0, 5), pl.ds(0, 1), pl.ds(0, 3)]
-        return pltpu.make_async_remote_copy(
-            src_ref=view, dst_ref=view, send_sem=wz_sems.at[0], recv_sem=wz_sems.at[1],
-            device_id={"fsdp": sibling}, device_id_type=MESH,
+    arrivals[-1].wait()
+    prepare(0)
+    my_slot = slot_of(dp, core)
+    w_own = pltpu.make_async_copy(
+        w_ref.at[
+            pl.ds(pl.multiple_of(q_part * w_rows, w_rows), w_rows),
+            pl.ds(pl.multiple_of(c_part * w_cols, w_cols), w_cols),
+        ],
+        wfull.at[chip // 4, (chip // 2) % 2, chip % 2, my_slot], own_sem.at[0],
+    )
+    w_own.start()
+    pl.semaphore_wait(barrier, n - 1 + (n_dp - 1))
+
+    def far_w(k):
+        away = (8, 4, 12)[k]
+        piece = wfull.at[chip // 4, (chip // 2) % 2, chip % 2, my_slot]
+        return pltpu.make_async_remote_copy(
+            src_ref=piece, dst_ref=piece, send_sem=wz_sems.at[0, k], recv_sem=wz_sems.at[1, k],
+            device_id={"fsdp": 2 * ((chip + away) % 16) + core}, device_id_type=MESH,
+        )
+
+    def near_w(k):
+        away = (2, 1, 15)[k]
+        pieces = wfull.at[:, (chip // 2) % 2, chip % 2, my_slot]
+        return pltpu.make_async_remote_copy(
+            src_ref=pieces, dst_ref=pieces, send_sem=wz_sems.at[2, k], recv_sem=wz_sems.at[3, k],
+            device_id={"fsdp": 2 * ((chip + away) % 16) + core}, device_id_type=MESH,
         )
 
     w_own.wait()
-    if q_parts * c_parts > 1:
-        ring_wait().wait_recv()
-    else:
-        @pl.loop(1, 16)
-        def _(i):
-            pltpu.make_async_remote_copy(
-                src_ref=w_mine(), dst_ref=w_place, send_sem=wz_sems.at[0], recv_sem=wz_sems.at[1],
-                device_id={"fsdp": sibling}, device_id_type=MESH,
-            ).wait_recv()
+    for k in range(3):
+        far_w(k).start()
+    send_some(0, 0, 16)
+    own_first = keep_own(0)
+    prepare(1)
+    for k in range(3):
+        far_w(k).wait_recv()
+    for k in range(3):
+        near_w(k).start()
+    send_some(0, 16, n - 1)
+
+    def group_of(peer):
+        return jnp.where(peer < 16, peer // 8, 2 + (peer - 16) // 4)
+
+    @pl.loop(0, n - 1)
+    def _(i):
+        peer = far_first(i)
+        pltpu.make_async_remote_copy(
+            src_ref=lab_send.at[group_of(peer)], dst_ref=lab_recv.at[me],
+            send_sem=lab_sems.at[0], recv_sem=lab_sems.at[1],
+            device_id={"fsdp": peer}, device_id_type=MESH,
+        ).start()
+
+    lab_own = pltpu.make_async_copy(lab_send.at[group_of(me)], lab_recv.at[me], own_sem.at[1])
+    lab_own.start()
+
+    own_second = keep_own(1)
+    for k in range(3):
+        near_w(k).wait_recv()
 
     def xy_copy(to, source):
-        part = wfull.at[:, :, slot_of(source, core)]
+        part = wfull.at[:, :, :, slot_of(source, core)]
         return pltpu.make_async_remote_copy(
             src_ref=part, dst_ref=part, send_sem=xy_send, recv_sem=xy_recv.at[source],
             device_id={"dp": to}, device_id_type=MESH,
@@ -241,15 +258,14 @@
             xy_copy((dp + i) % n_dp, dp).start()
 
     def sib_copy(source):
-        part = wfull.at[:, :, slot_of(source, core)]
+        part = wfull.at[:, :, :, slot_of(source, core)]
         return pltpu.make_async_remote_copy(
             src_ref=part, dst_ref=part, send_sem=sib_sems.at[0], recv_sem=sib_sems.at[1],
             device_id={"fsdp": sibling}, device_id_type=MESH,
         )
 
     sib_copy(dp).start()
-
-    own_second = prepare(1)
+    send_some(1, 0, n - 1)
 
     def label_wait():
         view = lab_recv.at[pl.ds(0, n - 1)]
@@ -286,9 +302,7 @@
         own_copy.wait()
         half_wait(half).wait_recv()
 
-        def block(step, carry):
-            turn = jnp.where(step == 0, 2, jnp.where(step == 1, 1, jnp.where(step == 2, 3, 0)))
-            part = (me // 8 + turn) % 4
+        def block(part, carry):
             first = pl.multiple_of(8 * part, 8)
             queries = jnp.concatenate(
                 [recv[half, pl.ds(first, 8), 0].reshape(256, HD),
@@ -308,20 +322,19 @@
             result = (total[:, :HD] / total[:, HD:]).astype(BF16)
             osend[half, pl.ds(first, 8)] = result.reshape(8, 32, HD)
 
-            @pl.loop(0, 8)
-            def _(i):
-                peer = first + (me + i) % 8
-
-                @pl.when(peer != me)
-                def _():
-                    pltpu.make_async_remote_copy(
-                        src_ref=osend.at[half, peer], dst_ref=orecv.at[half, me],
-                        send_sem=ret_send.at[half], recv_sem=ret_recv.at[half],
-                        device_id={"fsdp": peer}, device_id_type=MESH,
-                    ).start()
             return carry
 
         lax.fori_loop(0, 4, block, 0)
+
+        @pl.loop(0, n - 1)
+        def _(i):
+            peer = far_first(i)
+            pltpu.make_async_remote_copy(
+                src_ref=osend.at[half, peer], dst_ref=orecv.at[half, me],
+                send_sem=ret_send.at[half], recv_sem=ret_recv.at[half],
+                device_id={"fsdp": peer}, device_id_type=MESH,
+            ).start()
+
         copy = pltpu.make_async_copy(osend.at[half, me], orecv.at[half, me], own_sem.at[4 + half])
         copy.start()
         return copy
@@ -338,7 +351,7 @@
     back_second = attend(1, own_second)
 
     def sib_wait():
-        view = wfull.at[:, :, pl.ds(0, n_dp)]
+        view = wfull.at[:, :, :, pl.ds(0, n_dp)]
         return pltpu.make_async_remote_copy(
             src_ref=view, dst_ref=view, send_sem=sib_sems.at[0], recv_sem=sib_sems.at[1],
             device_id={"fsdp": sibling}, device_id_type=MESH,
@@ -356,7 +369,7 @@
         return jnp.concatenate(heads, axis=1)
 
     def project(half, c):
-        rows = wfull[:, half, 2 * q_parts * c:2 * q_parts * (c + 1)].reshape(8 * HD, w_cols)
+        rows = wfull[:, :, half, 2 * q_parts * c:2 * q_parts * (c + 1)].reshape(8 * HD, w_cols)
         return rows
 
     back_first.wait()
@@ -378,17 +391,13 @@
         half_wait(half).wait_send()
         back_wait(half).wait_send()
     label_wait().wait_send()
-    if q_parts * c_parts > 1:
-        ring_wait().wait_send()
-    else:
-        @pl.loop(1, 16)
-        def _(i):
-            pltpu.make_async_remote_copy(
-                src_ref=w_mine(), dst_ref=w_place, send_sem=wz_sems.at[0], recv_sem=wz_sems.at[1],
-                device_id={"fsdp": sibling}, device_id_type=MESH,
-            ).wait_send()
+    for k in range(3):
+        far_w(k).wait_send()
+    for k in range(3):
+        near_w(k).wait_send()
+
     if n_dp > 1:
-        view = wfull.at[:, :, pl.ds(0, n_dp - 1)]
+        view = wfull.at[:, :, :, pl.ds(0, n_dp - 1)]
         pltpu.make_async_remote_copy(
             src_ref=view, dst_ref=view, send_sem=xy_send, recv_sem=xy_recv.at[0],
             device_id={"fsdp": sibling}, device_id_type=MESH,
@@ -398,22 +407,31 @@
 
 def on_device(n_dp, projections, positions, packed_index, clip_length, clip_group, query_gain, key_gain, out_weight):
     q_parts, c_parts = {16: (4, 4), 2: (1, 2), 1: (1, 1)}[n_dp]
+    hbm = pl.BlockSpec(memory_space=pltpu.HBM)
     vmem = pl.BlockSpec(memory_space=pltpu.VMEM)
-    smem = pl.BlockSpec(memory_space=pltpu.SMEM)
     dma = pltpu.SemaphoreType.DMA
     return pl.pallas_call(
         functools.partial(kernel, n_dp, q_parts, c_parts),
         out_shape=jax.ShapeDtypeStruct((128, 1536), BF16),
-        in_specs=[vmem, vmem, vmem, smem, smem, vmem, vmem, vmem, vmem],
+        in_specs=[hbm] * 9,
         out_specs=vmem,
         scratch_shapes=[
+            pltpu.VMEM((3, 128, 2048), BF16),
+            pltpu.VMEM((3, 128), jnp.int32),
+            pltpu.VMEM((1, 128), jnp.int32),
+            pltpu.SMEM((CLIPS,), jnp.int32),
+            pltpu.SMEM((CLIPS,), jnp.int32),
+            pltpu.VMEM((1, HD), F32),
+            pltpu.VMEM((1, HD), F32),
+            pltpu.VMEM((8, HD), F32),
+            dma((8,)),
             pltpu.VMEM((2, 32, 3, 32, HD), BF16),
             pltpu.VMEM((2, 32, 3, 32, HD), BF16),
             pltpu.VMEM((GROUPS, 1, HD), F32),
             pltpu.VMEM((32, 1, HD), F32),
             pltpu.VMEM((2, 32, 32, HD), BF16),
             pltpu.VMEM((2, 32, 32, HD), BF16),
-            pltpu.VMEM((8, 2, 2 * q_parts * c_parts, 64 // q_parts, 1536 // c_parts), BF16),
+            pltpu.VMEM((4, 2, 2, 2 * q_parts * c_parts, 64 // q_parts, 1536 // c_parts), BF16),
             pltpu.VMEM((8 * HD, HD), BF16),
             pltpu.VMEM((8 * HD, HD), BF16),
             pltpu.VMEM((HD, HD), BF16),
@@ -424,13 +442,13 @@
             dma((2,)),
             dma((2,)),
             dma((6,)),
-            dma((2,)),
+            dma((4, 3)),
             dma,
             dma((n_dp,)),
             dma((2,)),
         ],
         compiler_params=pltpu.CompilerParams(
-            collective_id=0, has_side_effects=True, vmem_limit_bytes=40 * 1024 * 1024
+            collective_id=0, has_side_effects=True, vmem_limit_bytes=60 * 1024 * 1024
         ),
         cost_estimate=pl.CostEstimate(flops=3_500_000_000, bytes_accessed=4_000_000, transcendentals=2_500_000),
     )(

time: 128 us -> 118 us (0.922)
  local copies, waits for them, and re-layouts: 7.72 us -> 1.77 us
  Pallas kernels: 120 us -> 116 us
    unnamed x19 -> x1, local copies, waits for them, and re-layouts: 7.72 us -> 1.77 us
    pallas_call x1, Pallas kernels: 120 us -> 116 us  [on_device(): pl.pallas_call(functools.partial(kernel, n_dp, q_parts, c_parts), out_sha...]
where the time goes in v2:
time: 118 us
  Pallas kernels  116 us (98%)
  local copies, waits for them, and re-layouts  1.77 us (2%)
    pallas_call x1, Pallas kernels, on_device(): pl.pallas_call(functools.partial(kernel, n_dp, q_parts, c_parts), out_sha...  116 us

profile of v2, /device:TPU:1, one launch (start us, length us, event | category | flops | bytes accessed | tf_op | source)
XLA Modules:
  0.0 118.1 jit_solution(10069702813798153655)
XLA Ops:
  0.0 116.3 %shard_map.91 = bf16[128,1536]{1,0:T(8,128)(2,1)} custom-call(bf16[3,128,2048]{2,1,0:T(8,128)(2,1)} %bitcast.4, s32[3,128]{1,0:T(4,128)} %pos_hbm.1, s32[1,128]{1,0:T(1,128)} %bitcast.5, s32[24]{0:T(128)} %len_hbm.1, s32[24]{0:T(128)} %grp_hbm.1, f32[1,128]{1,0:T(1,128)} %bitcast.6, f32[1,128]{1,0:T(1,128)} %bitcast.7, bf16[64,1536]{1,0:T(8,128)(2,1)} %w_ref.1, ...), custom_call_target="tpu_custom_call" | custom-call | flops 3500000000 | bytes 4000000 | tf_op jit(solution)/shard_map/pallas_call | solution.py:413
  116.3 1.8 %copy.11 = bf16[128,1536]{1,0:T(8,128)(2,1)} copy(bf16[128,1536]{1,0:T(8,128)(2,1)} %shard_map.91) | data formatting | bytes 786432

commit v3 on v2

--- a/solution.py
+++ b/solution.py
@@ -48,7 +48,7 @@
     x_ref, pos_ref, idx_ref, len_ref, grp_ref, qg_ref, kg_ref, tab_ref, in_sems,
     send, recv, lab_send, lab_recv, osend, orecv, wfull, hot_q, hot_k, perm, acc,
     send_sem, recv_sem, lab_sems, ret_send, ret_recv, own_sem,
-    wz_sems, xy_send, xy_recv, sib_sems,
+    wz_sems, xy_send, xy_recv, sib_sems, ring_known, plane_known,
 ):
     n = 32
     dp = lax.axis_index("dp")
@@ -63,20 +63,31 @@
     def slot_of(row, side):
         return (row % c_parts) * (2 * q_parts) + side * q_parts + row // c_parts
 
-    def far_first(step):
-        near = n - 1 - step
-        return (me + jnp.where(near % 2 == 1, (near + 1) // 2, n - near // 2)) % n
+    def chip_at(away, side):
+        return 2 * ((chip + away + 16) % 16) + side
+
+    def near_first(i):
+        j = i + 3
+        away = jnp.where((j // 2) % 2 == 0, j // 4, -(j // 4))
+        return jnp.where(i == 0, sibling, chip_at(away, j % 2))
+
+    def far_first(i):
+        return near_first(n - 2 - i)
+
+    def tell(semaphore, **place):
+        pl.semaphore_signal(semaphore, inc=1, device_id=place, device_id_type=MESH)
 
     barrier = pltpu.get_barrier_semaphore()
 
-    @pl.loop(1, n)
-    def _(i):
-        pl.semaphore_signal(barrier, inc=1, device_id={"fsdp": (me + i) % n}, device_id_type=MESH)
-
-    if n_dp > 1:
-        @pl.loop(1, n_dp)
-        def _(i):
-            pl.semaphore_signal(barrier, inc=1, device_id={"dp": (dp + i) % n_dp}, device_id_type=MESH)
+    tell(barrier, fsdp=sibling)
+    for away in (1, -1):
+        for side in range(2):
+            tell(barrier, fsdp=chip_at(away, side))
+    if n_dp == 16:
+        row, column = dp // 4, dp % 4
+        for away in (1, 3):
+            tell(barrier, dp=4 * row + (column + away) % 4)
+            tell(barrier, dp=4 * ((row + away) % 4) + column)
 
     arrivals = [
         pltpu.make_async_copy(source, target, in_sems.at[i])
@@ -168,12 +179,12 @@
                     )
             return carry
 
-        lax.fori_loop(0, 8, one, 0)
-
-    def send_some(half, first, last):
+        lax.fori_loop(0, 8, one, 0, unroll=8)
+
+    def send_some(half, first, last, order=far_first):
         @pl.loop(first, last)
         def _(i):
-            peer = far_first(i)
+            peer = order(i)
             pltpu.make_async_remote_copy(
                 src_ref=send.at[half, peer], dst_ref=recv.at[half, me],
                 send_sem=send_sem.at[half], recv_sem=recv_sem.at[half],
@@ -196,35 +207,59 @@
         wfull.at[chip // 4, (chip // 2) % 2, chip % 2, my_slot], own_sem.at[0],
     )
     w_own.start()
-    pl.semaphore_wait(barrier, n - 1 + (n_dp - 1))
+    way = 1 - 2 * core
 
     def far_w(k):
-        away = (8, 4, 12)[k]
-        piece = wfull.at[chip // 4, (chip // 2) % 2, chip % 2, my_slot]
+        away = (4, 4, -4)[k] * way
+        origin = chip if k else (chip - 4 * way + 16) % 16
+        piece = wfull.at[origin // 4, (origin // 2) % 2, origin % 2, my_slot]
         return pltpu.make_async_remote_copy(
             src_ref=piece, dst_ref=piece, send_sem=wz_sems.at[0, k], recv_sem=wz_sems.at[1, k],
-            device_id={"fsdp": 2 * ((chip + away) % 16) + core}, device_id_type=MESH,
+            device_id={"fsdp": chip_at(away, core)}, device_id_type=MESH,
         )
 
     def near_w(k):
-        away = (2, 1, 15)[k]
+        away = (2, 1, -1)[k] * way
         pieces = wfull.at[:, (chip // 2) % 2, chip % 2, my_slot]
         return pltpu.make_async_remote_copy(
             src_ref=pieces, dst_ref=pieces, send_sem=wz_sems.at[2, k], recv_sem=wz_sems.at[3, k],
-            device_id={"fsdp": 2 * ((chip + away) % 16) + core}, device_id_type=MESH,
-        )
-
+            device_id={"fsdp": chip_at(away, core)}, device_id_type=MESH,
+        )
+
+    pl.semaphore_wait(barrier, 9 if n_dp == 16 else 5)
+    for away in (1, -1):
+        tell(ring_known.at[0], fsdp=chip_at(away, core))
+    send_some(0, 0, 5, near_first)
+    pl.semaphore_wait(ring_known.at[0], 2)
+    for away in (2, -2):
+        tell(ring_known.at[1], fsdp=chip_at(away, core))
+    send_some(0, 5, 9, near_first)
+    pl.semaphore_wait(ring_known.at[1], 2)
+    for away in (4, -4):
+        tell(ring_known.at[2], fsdp=chip_at(away, core))
     w_own.wait()
-    for k in range(3):
-        far_w(k).start()
-    send_some(0, 0, 16)
+    far_w(1).start()
+    far_w(2).start()
+    send_some(0, 9, 17, near_first)
     own_first = keep_own(0)
+    if n_dp == 16:
+        for away in (1, 3):
+            tell(plane_known.at[0], dp=4 * row + (column + away) % 4)
     prepare(1)
-    for k in range(3):
-        far_w(k).wait_recv()
+    own_second = keep_own(1)
+    far_w(1).wait_recv()
+    far_w(0).start()
+    pl.semaphore_wait(ring_known.at[2], 2)
+    send_some(0, 0, 2)
+    if n_dp == 16:
+        pl.semaphore_wait(plane_known.at[0], 2)
+        for away in (1, 3):
+            tell(plane_known.at[1], dp=4 * ((row + away) % 4) + column)
+    far_w(2).wait_recv()
+    far_w(0).wait_recv()
     for k in range(3):
         near_w(k).start()
-    send_some(0, 16, n - 1)
+    send_some(0, 2, 14)
 
     def group_of(peer):
         return jnp.where(peer < 16, peer // 8, 2 + (peer - 16) // 4)
@@ -241,7 +276,7 @@
     lab_own = pltpu.make_async_copy(lab_send.at[group_of(me)], lab_recv.at[me], own_sem.at[1])
     lab_own.start()
 
-    own_second = keep_own(1)
+    send_some(1, 0, 12)
     for k in range(3):
         near_w(k).wait_recv()
 
@@ -252,7 +287,11 @@
             device_id={"dp": to}, device_id_type=MESH,
         )
 
-    if n_dp > 1:
+    if n_dp == 16:
+        pl.semaphore_wait(plane_known.at[1], 2)
+        tell(plane_known.at[2], dp=4 * ((row + 2) % 4) + column)
+        pl.semaphore_wait(plane_known.at[2], 1)
+
         @pl.loop(1, n_dp)
         def _(i):
             xy_copy((dp + i) % n_dp, dp).start()
@@ -265,7 +304,7 @@
         )
 
     sib_copy(dp).start()
-    send_some(1, 0, n - 1)
+    send_some(1, 12, n - 1)
 
     def label_wait():
         view = lab_recv.at[pl.ds(0, n - 1)]
@@ -341,7 +380,7 @@
 
     back_first = attend(0, own_first)
 
-    if n_dp > 1:
+    if n_dp == 16:
         @pl.loop(1, n_dp)
         def _(i):
             source = (dp + n_dp - i) % n_dp
@@ -396,7 +435,7 @@
     for k in range(3):
         near_w(k).wait_send()
 
-    if n_dp > 1:
+    if n_dp == 16:
         view = wfull.at[:, :, :, pl.ds(0, n_dp - 1)]
         pltpu.make_async_remote_copy(
             src_ref=view, dst_ref=view, send_sem=xy_send, recv_sem=xy_recv.at[0],
@@ -406,7 +445,7 @@
 
 
 def on_device(n_dp, projections, positions, packed_index, clip_length, clip_group, query_gain, key_gain, out_weight):
-    q_parts, c_parts = {16: (4, 4), 2: (1, 2), 1: (1, 1)}[n_dp]
+    q_parts, c_parts = {16: (4, 4), 1: (1, 1)}[n_dp]
     hbm = pl.BlockSpec(memory_space=pltpu.HBM)
     vmem = pl.BlockSpec(memory_space=pltpu.VMEM)
     dma = pltpu.SemaphoreType.DMA
@@ -446,6 +485,8 @@
             dma,
             dma((n_dp,)),
             dma((2,)),
+            pltpu.SemaphoreType.REGULAR((3,)),
+            pltpu.SemaphoreType.REGULAR((3,)),
         ],
         compiler_params=pltpu.CompilerParams(
             collective_id=0, has_side_effects=True, vmem_limit_bytes=60 * 1024 * 1024

time: 118 us -> 116 us (0.983)
  Pallas kernels: 116 us -> 114 us
    pallas_call x1, Pallas kernels: 116 us -> 114 us  [on_device(): pl.pallas_call(functools.partial(kernel, n_dp, q_parts, c_parts), out_sha...]
where the time goes in v3:
time: 116 us; the launch traced here: 115 us
  Pallas kernels  114 us (98%)
  local copies, waits for them, and re-layouts  1.77 us (2%)
    pallas_call x1, Pallas kernels, on_device(): pl.pallas_call(functools.partial(kernel, n_dp, q_parts, c_parts), out_sha...  114 us

profile of v3, /device:TPU:1, one launch (start us, length us, event | category | flops | bytes accessed | tf_op | source)
XLA Modules:
  0.0 115.4 jit_solution(11129318727105935738)
XLA Ops:
  0.0 113.6 %shard_map.91 = bf16[128,1536]{1,0:T(8,128)(2,1)} custom-call(bf16[3,128,2048]{2,1,0:T(8,128)(2,1)} %bitcast.4, s32[3,128]{1,0:T(4,128)} %pos_hbm.1, s32[1,128]{1,0:T(1,128)} %bitcast.5, s32[24]{0:T(128)} %len_hbm.1, s32[24]{0:T(128)} %grp_hbm.1, f32[1,128]{1,0:T(1,128)} %bitcast.6, f32[1,128]{1,0:T(1,128)} %bitcast.7, bf16[64,1536]{1,0:T(8,128)(2,1)} %w_ref.1, ...), custom_call_target="tpu_custom_call" | custom-call | flops 3500000000 | bytes 4000000 | tf_op jit(solution)/shard_map/pallas_call | solution.py:452
  113.6 1.8 %copy.11 = bf16[128,1536]{1,0:T(8,128)(2,1)} copy(bf16[128,1536]{1,0:T(8,128)(2,1)} %shard_map.91) | data formatting | bytes 786432

commit v4 on v3

--- a/solution.py
+++ b/solution.py
@@ -68,7 +68,7 @@
 
     def near_first(i):
         j = i + 3
-        away = jnp.where((j // 2) % 2 == 0, j // 4, -(j // 4))
+        away = jnp.where((j // 2) % 2 == core, j // 4, -(j // 4))
         return jnp.where(i == 0, sibling, chip_at(away, j % 2))
 
     def far_first(i):
@@ -210,9 +210,8 @@
     way = 1 - 2 * core
 
     def far_w(k):
-        away = (4, 4, -4)[k] * way
-        origin = chip if k else (chip - 4 * way + 16) % 16
-        piece = wfull.at[origin // 4, (origin // 2) % 2, origin % 2, my_slot]
+        away = (8, 4, -4)[k] * way
+        piece = wfull.at[chip // 4, (chip // 2) % 2, chip % 2, my_slot]
         return pltpu.make_async_remote_copy(
             src_ref=piece, dst_ref=piece, send_sem=wz_sems.at[0, k], recv_sem=wz_sems.at[1, k],
             device_id={"fsdp": chip_at(away, core)}, device_id_type=MESH,
@@ -247,19 +246,19 @@
             tell(plane_known.at[0], dp=4 * row + (column + away) % 4)
     prepare(1)
     own_second = keep_own(1)
-    far_w(1).wait_recv()
+    send_some(1, 0, 9, near_first)
+    pl.semaphore_wait(ring_known.at[2], 2)
     far_w(0).start()
-    pl.semaphore_wait(ring_known.at[2], 2)
-    send_some(0, 0, 2)
+    send_some(0, 0, 3)
     if n_dp == 16:
         pl.semaphore_wait(plane_known.at[0], 2)
         for away in (1, 3):
             tell(plane_known.at[1], dp=4 * ((row + away) % 4) + column)
-    far_w(2).wait_recv()
-    far_w(0).wait_recv()
+    for k in range(3):
+        far_w(k).wait_recv()
     for k in range(3):
         near_w(k).start()
-    send_some(0, 2, 14)
+    send_some(0, 3, 14)
 
     def group_of(peer):
         return jnp.where(peer < 16, peer // 8, 2 + (peer - 16) // 4)
@@ -304,7 +303,7 @@
         )
 
     sib_copy(dp).start()
-    send_some(1, 12, n - 1)
+    send_some(1, 12, n - 10)
 
     def label_wait():
         view = lab_recv.at[pl.ds(0, n - 1)]

time: 116 us -> 115 us (level)
  no operation moved by 1% of the time
where the time goes in v4:
time: 115 us
  Pallas kernels  113 us (98%)
  local copies, waits for them, and re-layouts  1.77 us (2%)
    pallas_call x1, Pallas kernels, on_device(): pl.pallas_call(functools.partial(kernel, n_dp, q_parts, c_parts), out_sha...  113 us

profile of v4, /device:TPU:1, one launch (start us, length us, event | category | flops | bytes accessed | tf_op | source)
XLA Modules:
  0.0 115.3 jit_solution(12823555154640963532)
XLA Ops:
  0.0 113.5 %shard_map.91 = bf16[128,1536]{1,0:T(8,128)(2,1)} custom-call(bf16[3,128,2048]{2,1,0:T(8,128)(2,1)} %bitcast.4, s32[3,128]{1,0:T(4,128)} %pos_hbm.1, s32[1,128]{1,0:T(1,128)} %bitcast.5, s32[24]{0:T(128)} %len_hbm.1, s32[24]{0:T(128)} %grp_hbm.1, f32[1,128]{1,0:T(1,128)} %bitcast.6, f32[1,128]{1,0:T(1,128)} %bitcast.7, bf16[64,1536]{1,0:T(8,128)(2,1)} %w_ref.1, ...), custom_call_target="tpu_custom_call" | custom-call | flops 3500000000 | bytes 4000000 | tf_op jit(solution)/shard_map/pallas_call | solution.py:451
  113.5 1.8 %copy.11 = bf16[128,1536]{1,0:T(8,128)(2,1)} copy(bf16[128,1536]{1,0:T(8,128)(2,1)} %shard_map.91) | data formatting | bytes 786432

commit v5 on v4

--- a/solution.py
+++ b/solution.py
@@ -44,8 +44,8 @@
 def kernel(
     n_dp, q_parts, c_parts,
     x_hbm, pos_hbm, idx_hbm, len_hbm, grp_hbm, qg_hbm, kg_hbm, w_ref, tab_hbm,
-    out_ref,
-    x_ref, pos_ref, idx_ref, len_ref, grp_ref, qg_ref, kg_ref, tab_ref, in_sems,
+    out_hbm,
+    out_ref, out_sems, x_ref, pos_ref, idx_ref, len_ref, grp_ref, qg_ref, kg_ref, tab_ref, in_sems,
     send, recv, lab_send, lab_recv, osend, orecv, wfull, hot_q, hot_k, perm, acc,
     send_sem, recv_sem, lab_sems, ret_send, ret_recv, own_sem,
     wz_sems, xy_send, xy_recv, sib_sems, ring_known, plane_known,
@@ -424,6 +424,7 @@
         out_ref[:, columns] = jnp.dot(
             perm[...], mixed.astype(BF16), preferred_element_type=F32
         ).astype(BF16)
+        pltpu.make_async_copy(out_ref.at[:, columns], out_hbm.at[:, columns], out_sems.at[c]).start()
 
     for half in range(2):
         half_wait(half).wait_send()
@@ -441,19 +442,23 @@
             device_id={"fsdp": sibling}, device_id_type=MESH,
         ).wait_send()
     sib_wait().wait_send()
+    for c in range(c_parts):
+        columns = slice(c * w_cols, (c + 1) * w_cols)
+        pltpu.make_async_copy(out_ref.at[:, columns], out_hbm.at[:, columns], out_sems.at[c]).wait()
 
 
 def on_device(n_dp, projections, positions, packed_index, clip_length, clip_group, query_gain, key_gain, out_weight):
     q_parts, c_parts = {16: (4, 4), 1: (1, 1)}[n_dp]
     hbm = pl.BlockSpec(memory_space=pltpu.HBM)
-    vmem = pl.BlockSpec(memory_space=pltpu.VMEM)
     dma = pltpu.SemaphoreType.DMA
     return pl.pallas_call(
         functools.partial(kernel, n_dp, q_parts, c_parts),
         out_shape=jax.ShapeDtypeStruct((128, 1536), BF16),
         in_specs=[hbm] * 9,
-        out_specs=vmem,
+        out_specs=hbm,
         scratch_shapes=[
+            pltpu.VMEM((128, 1536), BF16),
+            dma((c_parts,)),
             pltpu.VMEM((3, 128, 2048), BF16),
             pltpu.VMEM((3, 128), jnp.int32),
             pltpu.VMEM((1, 128), jnp.int32),

time: 115 us -> 115 us (level)
  no operation moved by 1% of the time
where the time goes in v5:
time: 115 us
  Pallas kernels  113 us (98%)
  local copies, waits for them, and re-layouts  1.77 us (2%)
    pallas_call x1, Pallas kernels, on_device(): pl.pallas_call(functools.partial(kernel, n_dp, q_parts, c_parts), out_sha...  113 us

profile of v5, /device:TPU:1, one launch (start us, length us, event | category | flops | bytes accessed | tf_op | source)
XLA Modules:
  0.0 115.2 jit_solution(2632693713512018955)
XLA Ops:
  0.0 113.4 %shard_map.91 = bf16[128,1536]{1,0:T(8,128)(2,1)} custom-call(bf16[3,128,2048]{2,1,0:T(8,128)(2,1)} %bitcast.4, s32[3,128]{1,0:T(4,128)} %pos_hbm.1, s32[1,128]{1,0:T(1,128)} %bitcast.5, s32[24]{0:T(128)} %len_hbm.1, s32[24]{0:T(128)} %grp_hbm.1, f32[1,128]{1,0:T(1,128)} %bitcast.6, f32[1,128]{1,0:T(1,128)} %bitcast.7, bf16[64,1536]{1,0:T(8,128)(2,1)} %w_ref.1, ...), custom_call_target="tpu_custom_call" | custom-call | flops 3500000000 | bytes 4000000 | tf_op jit(solution)/shard_map/pallas_call | solution.py:454
  113.4 1.8 %copy.11 = bf16[128,1536]{1,0:T(8,128)(2,1)} copy(bf16[128,1536]{1,0:T(8,128)(2,1)} %shard_map.91) | data formatting | bytes 786432
